TPU v7x, 128 devices: a whole 4x4x4 slice. The times are simulated.
128 devices in a mesh: gx: 8 (over y, core), gy: 16 (over x, z).
Axes of the slice: x: 4, y: 4, z: 4, core: 2. Of those that a mesh axis runs over, the one named last changes fastest.
Arguments:
- item_table: bfloat16 [2097152, 128], P(('gx', 'gy'))
- block_ids: int32 [16384, 8], P(('gx', 'gy')), may hold values from 0 to 262143, as said below
- item_slots: int32 [16384, 32], P(('gx', 'gy')), may hold values from 0 to 7
- item_offsets: int32 [16384, 32], P(('gx', 'gy')), may hold values from 0 to 7
- confidence: float32 [16384, 32], P(('gx', 'gy')), may hold values from 0.5 to 4
- item_counts: int32 [16384], P(('gx', 'gy')), may hold values from 8 to 32
- owner_map: int32 [262144], replicated, may hold values from 0 to 262143, as said below
Outputs:
- user_factors: float32 [16384, 128], P(('gx', 'gy'))
Inputs may be any that keep to these rules, and one draw needn't show every extreme that they name: `block_ids`: each device's users (128 rows, 8 slots each) name at most 16 blocks b whose storage block owner_map[b] lies on any one device (owner_map[b] // 2048); one device holds exactly 16 of the named blocks of every device's users. `owner_map`: A permutation of the block numbers.
All inputs are finite; a program needn't handle non-finite values.
Results may differ from a plain program's by a relative error of at most 0.0014.
Values may be sent and summed in bfloat16 or wider, within the bound.
A program may use at most 64 MiB of HBM per device.

v0:
```python
import functools

import jax
import jax.numpy as jnp
from jax import lax
from jax.experimental import pallas as pl
from jax.experimental.pallas import tpu as pltpu
from jax.sharding import PartitionSpec as P

BLOCK = 8
USER_BLOCKS = 8
USER_ITEMS = 32
ITERATIONS = 16
LANES = 128
CORES = 2
RING = 4
ROOM = 48
CHIP_ROOM = CORES * ROOM
MOST = 128
MARK = 1 << 20

MESH = pl.DeviceIdType.MESH
F32 = jnp.float32
BF16 = jnp.bfloat16
VMEM_LIMIT = 56 * 1024 * 1024


def place(gy_size):
    gx, gy = lax.axis_index("gx"), lax.axis_index("gy")
    return gx * gy_size + gy


def signal_all(me, shards, gy_size):
    barrier = pltpu.get_barrier_semaphore()

    def one(i, carry):
        peer = lax.rem(me + i, shards)
        pl.semaphore_signal(
            barrier,
            inc=1,
            device_id=(peer // gy_size, lax.rem(peer, gy_size)),
            device_id_type=MESH,
        )
        return carry

    lax.fori_loop(1, shards, one, 0)
    return barrier


def send(src, dst, send_sem, recv_sem, peer, gy_size):
    return pltpu.make_async_remote_copy(
        src_ref=src,
        dst_ref=dst,
        send_sem=send_sem,
        recv_sem=recv_sem,
        device_id=(peer // gy_size, lax.rem(peer, gy_size)),
        device_id_type=MESH,
    )


def exchange_rows(table, landing, me, shards, gy_size, send_sem, recv_sem):
    def one(i, carry):
        peer = lax.rem(me + i, shards)
        send(table.at[peer], landing.at[me], send_sem, recv_sem, peer, gy_size).start()
        return carry

    lax.fori_loop(1, shards, one, 0)


def await_rows(table, landing, shards, gy_size, send_sem, recv_sem):
    others = pl.ds(0, shards - 1)
    send(table.at[others], landing.at[others], send_sem, recv_sem, 0, gy_size).wait()


def ask_kernel(
    shards, gy_size, blocks_dev, ids, owner_map, need, asked, keys, top,
    owners, found, queries, map_sem, own_sem, send_sem, recv_sem,
):
    me = place(gy_size)
    barrier = signal_all(me, shards, gy_size)
    load = pltpu.make_async_copy(owner_map, owners, map_sem)
    load.start()
    requests = found.shape[0]
    lane_row = lax.broadcasted_iota(jnp.int32, (1, LANES), 1)
    load.wait()

    def look(j, carry):
        for t in range(8):
            i = j * 8 + t
            block = ids[i // LANES, lax.rem(i, LANES)]
            row = owners[pl.ds(lax.shift_right_logical(block, 7), 1), :]
            found[pl.ds(i, 1), :] = jnp.where(lane_row == (block & (LANES - 1)), row, 0)
        return carry

    lax.fori_loop(0, requests // 8, look, 0)

    chunk = LANES
    lane = lax.broadcasted_iota(jnp.int32, (chunk, LANES), 1)
    sub = lax.broadcasted_iota(jnp.int32, (chunk, LANES), 0)
    lane8 = lax.broadcasted_iota(jnp.int32, (chunk, BLOCK), 1)
    earlier = jnp.where(lane < sub, 1.0, 0.0).astype(BF16)
    total = jnp.zeros((1, LANES), F32)
    low = jnp.zeros((LANES, LANES), F32)
    high = jnp.zeros((LANES, LANES), F32)
    over_rows = (((0,), (0,)), ((), ()))
    for a in range(requests // chunk):
        rows = pl.ds(a * chunk, chunk)
        storage = jnp.sum(found[rows, :].astype(F32), axis=1, keepdims=True).astype(jnp.int32)
        owner = storage // blocks_dev
        within = storage - owner * blocks_dev
        wanted = need[rows, :]
        count = jnp.sum(wanted, axis=1, keepdims=True)
        mine = owner == lane
        one_hot = jnp.where(mine, 1.0, 0.0).astype(BF16)
        counted = jnp.where(mine, count, 0.0)
        before = jnp.dot(earlier, counted.astype(BF16), preferred_element_type=F32) + total
        start = jnp.sum(jnp.where(mine, before, 0.0), axis=1, keepdims=True).astype(jnp.int32)
        total = total + jnp.sum(counted, axis=0, keepdims=True)
        first = within * BLOCK
        low_here = jnp.zeros((chunk, LANES), F32)
        high_here = jnp.zeros((chunk, LANES), F32)
        key = jnp.zeros((chunk, BLOCK), jnp.int32)
        for r in range(BLOCK):
            live = wanted[:, r : r + 1]
            row = first + r
            hit = jnp.where(lane == start, live, 0.0)
            low_here = low_here + hit * (row & (LANES - 1)).astype(F32)
            high_here = high_here + hit * lax.shift_right_logical(row, 7).astype(F32)
            spot = jnp.where(live > 0.0, owner * MOST + start, 0)
            key = jnp.where(lane8 == r, spot, key)
            start = start + live.astype(jnp.int32)
        keys[rows, :] = key
        low = low + lax.dot_general(
            one_hot, low_here.astype(BF16), over_rows, preferred_element_type=F32
        )
        high = high + lax.dot_general(
            one_hot, high_here.astype(BF16), over_rows, preferred_element_type=F32
        )
    most = jnp.max(total, axis=1, keepdims=True)
    mark = jnp.where(most > MOST, float(MARK), 0.0)
    query = (low + high * float(LANES) + mark).astype(jnp.int32)
    for o in range(shards):
        queries[o] = query[o : o + 1, :]

    pl.semaphore_wait(barrier, shards - 1)
    exchange_rows(queries, asked, me, shards, gy_size, send_sem, recv_sem)
    own = pltpu.make_async_copy(queries.at[me], asked.at[me], own_sem)
    own.start()
    own.wait()
    await_rows(queries, asked, shards, gy_size, send_sem, recv_sem)
    top[...] = jnp.max(jnp.max(asked[...], axis=0), axis=1, keepdims=True)


def fetch_kernel(
    shards, gy_size, room, asked, table, landed, gramian,
    packed, wide, stage, outgoing, terms, arrived, row_total, table_sem, own_sem,
    send_sem, recv_sem, term_send, term_recv, sum_send, sum_recv,
):
    me = place(gy_size)
    barrier = signal_all(me, shards, gy_size)
    rows_dev = table.shape[0]
    parts = 8
    part = rows_dev // parts

    def load(c):
        rows = pl.ds(c * part, part)
        return pltpu.make_async_copy(table.at[rows], packed.at[rows], table_sem.at[c])

    for c in range(parts):
        load(c).start()
    piece = min(512, part)
    total = jnp.zeros((LANES, LANES), F32)
    for c in range(parts):
        load(c).wait()

        def step(j, total):
            rows = pl.ds(pl.multiple_of(c * part + j * piece, piece), piece)
            block = packed[rows, :]
            wide[rows, :] = block.astype(F32)
            return total + lax.dot_general(
                block, block, (((0,), (0,)), ((), ())), preferred_element_type=F32
            )

        total = lax.fori_loop(0, part // piece, step, total)
    for o in range(shards):
        terms[o] = total[o : o + 1, :]

    pl.semaphore_wait(barrier, shards - 1)
    exchange_rows(terms, arrived, me, shards, gy_size, term_send, term_recv)
    own_term = pltpu.make_async_copy(terms.at[me], arrived.at[me], own_sem.at[0])
    own_term.start()

    def collect(peer):
        for h in range(room // 16):
            for t in range(16):
                row = asked[peer, h * 16 + t] & (rows_dev - 1)
                stage[pl.ds(h * 16 + t, 1), :] = wide[pl.ds(row, 1), :]
        outgoing[peer] = stage[...].astype(BF16)

    def serve(i, carry):
        off = lax.rem(i * 37, shards)
        peer = lax.rem(me + off, shards)
        collect(peer)
        send(outgoing.at[peer], landed.at[me], send_sem, recv_sem, peer, gy_size).start()
        return carry

    lax.fori_loop(1, shards // 2, serve, 0)
    own_term.wait()
    await_rows(terms, arrived, shards, gy_size, term_send, term_recv)
    row_total[...] = jnp.sum(arrived[...], axis=0)

    def share(i, carry):
        peer = lax.rem(me + i, shards)
        send(row_total, gramian.at[me], sum_send, sum_recv, peer, gy_size).start()
        return carry

    lax.fori_loop(1, shards, share, 0)
    own_sum = pltpu.make_async_copy(row_total, gramian.at[me], own_sem.at[1])
    own_sum.start()
    lax.fori_loop(shards // 2, shards, serve, 0)
    collect(me)
    own = pltpu.make_async_copy(outgoing.at[me], landed.at[me], own_sem.at[2])
    own.start()
    own_sum.wait()
    own.wait()
    await_rows(terms, gramian, shards, gy_size, sum_send, sum_recv)
    await_rows(outgoing, landed, shards, gy_size, send_sem, recv_sem)


def bits(count):
    assert count & (count - 1) == 0
    return count.bit_length() - 1


def chip_of(device, gy_size):
    gx, gy = device // gy_size, lax.rem(device, gy_size)
    return (gx // CORES) * gy_size + gy, lax.rem(gx, CORES)


def shifted(me, off, gy_size):
    gx, gy = me // gy_size, lax.rem(me, gy_size)
    y, core, x, z = gx // CORES, lax.rem(gx, CORES), gy // RING, lax.rem(gy, RING)
    z = lax.rem(z + lax.rem(off, RING), RING)
    x = lax.rem(x + lax.rem(off // RING, RING), RING)
    core = lax.rem(core + lax.rem(off // (RING * RING), CORES), CORES)
    y = lax.rem(y + off // (RING * RING * CORES), RING)
    return (y * CORES + core) * gy_size + x * RING + z


def gather_kernel(
    shards, gy_size, blocks_dev, ids, id_rows, owner_map, slots, offsets, counts, table,
    landed, gramian, spots, top,
    owners, found, queries, asked, asked_here, packed, twin_packed, wide, stage, outgoing,
    terms, arrived, row_total, load_sem, own_sem, table_send, table_recv,
    send_sem, recv_sem, ask_send, ask_recv, term_send, term_recv, sum_send, sum_recv,
):
    me = place(gy_size)
    chip_me, core_me = chip_of(me, gy_size)
    barrier = signal_all(me, shards, gy_size)
    load_map = pltpu.make_async_copy(owner_map, owners, own_sem.at[0])
    load_map.start()
    rows_dev = table.shape[0]
    parts = 8
    part = rows_dev // parts

    def load(c):
        rows = pl.ds(c * part, part)
        return pltpu.make_async_copy(table.at[rows], packed.at[rows], load_sem.at[c])

    for c in range(parts):
        load(c).start()

    users = slots.shape[0]
    requests = found.shape[0]
    group = LANES // USER_BLOCKS
    lane = lax.broadcasted_iota(jnp.int32, (LANES, LANES), 1)
    sub = lax.broadcasted_iota(jnp.int32, (LANES, LANES), 0)
    lane_f = lane.astype(F32)
    diagonal = lane == sub

    count = jnp.sum(jnp.where(diagonal, counts[...], 0).astype(F32), axis=1, keepdims=True)
    slot_lane = lax.broadcasted_iota(jnp.int32, (users, USER_ITEMS), 1)
    row_index = slots[...] * BLOCK + offsets[...]
    row_index = jnp.where(slot_lane < count.astype(jnp.int32), row_index, -1)
    wanted = lane == row_index[:, 0:1]
    for item in range(1, USER_ITEMS):
        wanted = wanted | (lane == row_index[:, item : item + 1])
    wanted = jnp.where(wanted, 1.0, 0.0).astype(BF16)
    inner = jnp.zeros((users, LANES), F32)
    for slot in range(USER_BLOCKS):
        id_low = (id_rows[:, slot : slot + 1] & (LANES - 1)).astype(F32)
        inner = jnp.where(lane == slot, id_low, inner)
    inner = inner.astype(BF16)

    load_map.wait()

    def look(user, carry):
        for slot in range(USER_BLOCKS):
            line = lax.shift_right_logical(ids[user, slot], bits(LANES))
            found[pl.ds(user * USER_BLOCKS + slot, 1), :] = owners[pl.ds(line, 1), :]
        return carry

    lax.fori_loop(0, users, look, 0, unroll=2)

    same = lax.shift_right_logical(lane, 3) == (sub & 7)
    own_lane = lane == (sub & 7)
    earlier = jnp.where(lane < sub, 1.0, 0.0).astype(BF16)
    before_row = jnp.where(
        (lax.shift_right_logical(lane, 3) == lax.shift_right_logical(sub, 3))
        & ((sub & 7) < (lane & 7)),
        1.0,
        0.0,
    ).astype(BF16)
    up_to = [jnp.where((sub & 7) <= r, 1.0, 0.0).astype(BF16) for r in range(BLOCK)]
    total = jnp.zeros((1, LANES), F32)
    low_high = jnp.zeros((LANES, 2 * LANES), F32)
    pos_chip = jnp.zeros((users, 2 * LANES), F32)
    for a in range(requests // LANES):
        pick = jnp.where(sub // USER_BLOCKS + a * group == lane, 1.0, 0.0).astype(BF16)
        place_back = jnp.where(lane // USER_BLOCKS + a * group == sub, 1.0, 0.0).astype(BF16)
        spread = jnp.dot(pick, wanted, preferred_element_type=F32)
        spread = jnp.where(same, spread, 0.0)
        live = spread > 0.0
        spread = spread.astype(BF16)
        inner_here = jnp.dot(pick, inner, preferred_element_type=F32)
        inner_here = jnp.sum(jnp.where(own_lane, inner_here, 0.0), axis=1, keepdims=True)
        line = found[pl.ds(a * LANES, LANES), :].astype(F32)
        storage = jnp.sum(jnp.where(lane_f == inner_here, line, 0.0), axis=1, keepdims=True)
        storage = storage.astype(jnp.int32)
        device = lax.shift_right_logical(storage, bits(blocks_dev))
        within = storage & (blocks_dev - 1)
        gx = lax.shift_right_logical(device, bits(gy_size))
        chip = lax.shift_right_logical(gx, bits(CORES)) * gy_size + (device & (gy_size - 1))
        core = gx & (CORES - 1)
        low_first = ((within & 15) * BLOCK).astype(F32)
        high = (core * (rows_dev // LANES) + lax.shift_right_logical(within, 4)).astype(F32)
        chip = chip.astype(F32)
        so_far = [jnp.dot(spread, m, preferred_element_type=F32) for m in up_to]
        mine = lane_f == chip
        counted = jnp.where(mine, so_far[-1], 0.0)
        before = jnp.dot(earlier, counted.astype(BF16), preferred_element_type=F32) + total
        start = jnp.sum(jnp.where(mine, before, 0.0), axis=1, keepdims=True)
        total = total + jnp.sum(counted, axis=0, keepdims=True)
        depth = lane_f - start
        which = jnp.zeros((LANES, LANES), F32)
        for m in so_far:
            which = which + jnp.where(m <= depth, 1.0, 0.0)
        hit = (depth >= 0.0) & (depth < so_far[-1])
        both = jnp.concatenate(
            [jnp.where(hit, low_first + which, 0.0), jnp.where(hit, high, 0.0)], axis=1
        ).astype(BF16)
        chip_row = jnp.sum(jnp.where(diagonal, chip, 0.0), axis=0, keepdims=True)
        to_chip = jnp.where(sub.astype(F32) == chip_row, 1.0, 0.0).astype(BF16)
        low_high = low_high + jnp.dot(to_chip, both, preferred_element_type=F32)
        spot = jnp.dot(spread, before_row, preferred_element_type=F32) + start
        both = jnp.concatenate(
            [jnp.where(live, spot, 0.0), jnp.where(live, chip, 0.0)], axis=1
        ).astype(BF16)
        pos_chip = pos_chip + jnp.dot(place_back, both, preferred_element_type=F32)
    most = jnp.max(total, axis=1, keepdims=True)
    mark = jnp.where(most > CHIP_ROOM, float(MARK), 0.0)
    query = (low_high[:, :LANES] + low_high[:, LANES:] * float(LANES) + mark).astype(jnp.int32)
    for o in range(shards // CORES):
        queries[o] = query[o : o + 1, :]

    pl.semaphore_wait(barrier, shards - 1)
    twin = shifted(me, RING * RING, gy_size)
    lend = send(table, twin_packed, table_send, table_recv, twin, gy_size)
    lend.start()

    def ask_one(i, carry):
        peer = lax.rem(me + i, shards)
        chip, _ = chip_of(peer, gy_size)
        send(queries.at[chip], asked.at[me], ask_send, ask_recv, peer, gy_size).start()
        return carry

    lax.fori_loop(1, shards, ask_one, 0)
    own_ask = pltpu.make_async_copy(queries.at[chip_me], asked.at[me], own_sem.at[1])
    own_ask.start()

    piece = min(512, part)
    gram = jnp.zeros((LANES, LANES), F32)
    mine_from = core_me * rows_dev
    for c in range(parts):
        load(c).wait()

        def step(j, gram):
            at = c * part + j * piece
            block = packed[pl.ds(pl.multiple_of(at, piece), piece), :]
            wide[pl.ds(pl.multiple_of(mine_from + at, piece), piece), :] = block.astype(F32)
            return gram + lax.dot_general(
                block, block, (((0,), (0,)), ((), ())), preferred_element_type=F32
            )

        gram = lax.fori_loop(0, part // piece, step, gram)
    for o in range(LANES):
        terms[o] = gram[o : o + 1, :]
    exchange_rows(terms, arrived, me, shards, gy_size, term_send, term_recv)
    own_term = pltpu.make_async_copy(terms.at[me], arrived.at[me], own_sem.at[2])
    own_term.start()

    own_ask.wait()
    await_rows(asked, asked, shards, gy_size, ask_send, ask_recv)
    to_scalars = pltpu.make_async_copy(asked, asked_here, own_sem.at[3])
    to_scalars.start()
    lend.wait()
    theirs_from = (CORES - 1 - core_me) * rows_dev

    def widen(j, carry):
        at = j * piece
        block = twin_packed[pl.ds(pl.multiple_of(at, piece), piece), :]
        wide[pl.ds(pl.multiple_of(theirs_from + at, piece), piece), :] = block.astype(F32)
        return carry

    lax.fori_loop(0, rows_dev // piece, widen, 0)
    to_scalars.wait()

    my_part = core_me * ROOM
    my_place = chip_me * CORES + core_me

    def collect(peer):
        for t in range(ROOM):
            row = asked_here[peer, 0, my_part + t] & (CORES * rows_dev - 1)
            stage[pl.ds(t, 1), :] = wide[pl.ds(row, 1), :]
        outgoing[peer] = stage[...].astype(BF16)

    def serve(i, carry):
        peer = shifted(me, lax.rem(i * 37, shards), gy_size)
        collect(peer)
        send(outgoing.at[peer], landed.at[my_place], send_sem, recv_sem, peer, gy_size).start()
        return carry

    lax.fori_loop(1, shards // 2, serve, 0)
    own_term.wait()
    await_rows(terms, arrived, shards, gy_size, term_send, term_recv)
    row_total[...] = jnp.sum(arrived[...], axis=0)

    def share(i, carry):
        peer = lax.rem(me + i, shards)
        send(row_total, gramian.at[me], sum_send, sum_recv, peer, gy_size).start()
        return carry

    lax.fori_loop(1, shards, share, 0)
    own_sum = pltpu.make_async_copy(row_total, gramian.at[me], own_sem.at[4])
    own_sum.start()
    lax.fori_loop(shards // 2, shards, serve, 0)
    collect(me)
    own = pltpu.make_async_copy(outgoing.at[me], landed.at[my_place], own_sem.at[5])
    own.start()

    spot = pos_chip[:, :LANES] + pos_chip[:, LANES:] * float(CHIP_ROOM)
    spots_now = jnp.zeros((users, USER_ITEMS), F32)
    for item in range(USER_ITEMS):
        chosen = jnp.where(lane == row_index[:, item : item + 1], spot, 0.0)
        chosen = jnp.sum(chosen, axis=1, keepdims=True)
        spots_now = jnp.where(slot_lane == item, chosen, spots_now)
    spots[...] = spots_now.astype(jnp.int32)
    top[...] = jnp.max(jnp.max(asked[...], axis=0), axis=1, keepdims=True)

    own_sum.wait()
    own.wait()
    await_rows(terms, gramian, shards, gy_size, sum_send, sum_recv)
    await_rows(outgoing, landed, shards, gy_size, send_sem, recv_sem)


def solve_kernel(
    unobserved, spots, landed, gramian, confidence, counts, out, packed, wide, rows, vectors, weights, sem
):
    users = confidence.shape[0]
    parts = 8
    part = landed.shape[0] // parts

    def load(c):
        here = pl.ds(c * part, part)
        return pltpu.make_async_copy(landed.at[here], packed.at[here], sem.at[c])

    for c in range(parts):
        load(c).start()
    for c in range(parts):
        load(c).wait()
        here = pl.ds(c * part, part)
        wide[here, :] = packed[here, :].astype(F32)

    def pick(user, carry):
        for item in range(USER_ITEMS):
            rows[pl.ds(item * users + user, 1), :] = wide[pl.ds(spots[user, item], 1), :]
        return carry

    lax.fori_loop(0, users, pick, 0)
    unit = jnp.where(
        lax.broadcasted_iota(jnp.int32, (LANES, LANES), 0)
        == lax.broadcasted_iota(jnp.int32, (LANES, LANES), 1),
        1.0,
        0.0,
    ).astype(BF16)
    for item in range(USER_ITEMS):
        block = rows[pl.ds(item * users, users), :].astype(BF16)
        vectors[item] = lax.dot_general(
            unit, block, (((1,), (1,)), ((), ())), preferred_element_type=F32
        )

    item_sub = lax.broadcasted_iota(jnp.int32, (USER_ITEMS, users), 0)
    weights[...] = jnp.where(item_sub < counts[...], confidence[...].T, 0.0)
    scaled = gramian[...] * unobserved
    top = scaled.astype(BF16)
    rest = (scaled - top.astype(F32)).astype(BF16)

    right = jnp.zeros((LANES, users), F32)
    for item in range(USER_ITEMS):
        right = right + vectors[item] * weights[item : item + 1, :]
    norm = jnp.sum(right * right, axis=0, keepdims=True)

    def sweep(_, carry):
        solution, residual, direction, norm = carry
        d_top = direction.astype(BF16)
        d_rest = (direction - d_top.astype(F32)).astype(BF16)
        image = direction + (
            jnp.dot(top, d_top, preferred_element_type=F32)
            + jnp.dot(top, d_rest, preferred_element_type=F32)
            + jnp.dot(rest, d_top, preferred_element_type=F32)
        )
        for item in range(USER_ITEMS):
            vector = vectors[item]
            projected = jnp.sum(vector * direction, axis=0, keepdims=True)
            image = image + vector * (weights[item : item + 1, :] * projected)
        alpha = norm / jnp.sum(direction * image, axis=0, keepdims=True)
        solution = solution + alpha * direction
        residual = residual - alpha * image
        after = jnp.sum(residual * residual, axis=0, keepdims=True)
        direction = residual + (after / norm) * direction
        return solution, residual, direction, after

    solution, *_ = lax.fori_loop(
        0, ITERATIONS, sweep, (jnp.zeros_like(right), right, right, norm)
    )
    out[...] = solution.T


def vmem():
    return pl.BlockSpec(memory_space=pltpu.VMEM)


def smem():
    return pl.BlockSpec(memory_space=pltpu.SMEM)


def anywhere():
    return pl.BlockSpec(memory_space=pl.ANY)


def ask(shards, gy_size, blocks_dev, ids, owner_map, need):
    requests = need.shape[0]
    dma = pltpu.SemaphoreType.DMA
    return pl.pallas_call(
        functools.partial(ask_kernel, shards, gy_size, blocks_dev),
        out_shape=(
            jax.ShapeDtypeStruct((shards, 1, LANES), jnp.int32),
            jax.ShapeDtypeStruct((requests, BLOCK), jnp.int32),
            jax.ShapeDtypeStruct((1, 1), jnp.int32),
        ),
        in_specs=[smem(), anywhere(), vmem()],
        out_specs=(vmem(), vmem(), vmem()),
        scratch_shapes=[
            pltpu.VMEM(owner_map.shape, jnp.int32),
            pltpu.VMEM((requests, LANES), jnp.int32),
            pltpu.VMEM((shards, 1, LANES), jnp.int32),
            dma, dma, dma, dma,
        ],
        compiler_params=pltpu.CompilerParams(
            collective_id=1, has_side_effects=True, vmem_limit_bytes=VMEM_LIMIT
        ),
        name="ask",
    )(ids, owner_map, need)


def fetch(shards, gy_size, room, asked, table):
    dma = pltpu.SemaphoreType.DMA
    return pl.pallas_call(
        functools.partial(fetch_kernel, shards, gy_size, room),
        out_shape=(
            jax.ShapeDtypeStruct((shards, room, LANES), BF16),
            jax.ShapeDtypeStruct((shards, 1, LANES), F32),
        ),
        in_specs=[smem(), anywhere()],
        out_specs=(anywhere(), vmem()),
        scratch_shapes=[
            pltpu.VMEM(table.shape, BF16),
            pltpu.VMEM(table.shape, F32),
            pltpu.VMEM((room, LANES), F32),
            pltpu.VMEM((shards, room, LANES), BF16),
            pltpu.VMEM((shards, 1, LANES), F32),
            pltpu.VMEM((shards, 1, LANES), F32),
            pltpu.VMEM((1, LANES), F32),
            pltpu.SemaphoreType.DMA((8,)),
            pltpu.SemaphoreType.DMA((3,)),
            dma, dma, dma, dma, dma, dma,
        ],
        compiler_params=pltpu.CompilerParams(
            collective_id=2,
            has_side_effects=True,
            vmem_limit_bytes=VMEM_LIMIT,
        ),
        name="fetch",
    )(asked, table)


def gather(shards, gy_size, blocks_dev, block_ids, owner_map, slots, offsets, counts, table):
    dma = pltpu.SemaphoreType.DMA
    users = slots.shape[0]
    line = (shards, 1, LANES)
    return pl.pallas_call(
        functools.partial(gather_kernel, shards, gy_size, blocks_dev),
        out_shape=(
            jax.ShapeDtypeStruct((shards, ROOM, LANES), BF16),
            jax.ShapeDtypeStruct(line, F32),
            jax.ShapeDtypeStruct((users, USER_ITEMS), jnp.int32),
            jax.ShapeDtypeStruct((1, 1), jnp.int32),
        ),
        in_specs=[smem(), vmem(), anywhere(), vmem(), vmem(), vmem(), anywhere()],
        out_specs=(anywhere(), vmem(), vmem(), vmem()),
        scratch_shapes=[
            pltpu.VMEM(owner_map.shape, jnp.int32),
            pltpu.VMEM((users * USER_BLOCKS, LANES), jnp.int32),
            pltpu.VMEM((shards // CORES, 1, LANES), jnp.int32),
            pltpu.VMEM(line, jnp.int32),
            pltpu.SMEM(line, jnp.int32),
            pltpu.VMEM(table.shape, BF16),
            pltpu.VMEM(table.shape, BF16),
            pltpu.VMEM((CORES * table.shape[0], LANES), F32),
            pltpu.VMEM((ROOM, LANES), F32),
            pltpu.VMEM((shards, ROOM, LANES), BF16),
            pltpu.VMEM(line, F32),
            pltpu.VMEM(line, F32),
            pltpu.VMEM((1, LANES), F32),
            pltpu.SemaphoreType.DMA((8,)),
            pltpu.SemaphoreType.DMA((6,)),
            dma, dma, dma, dma, dma, dma, dma, dma, dma, dma,
        ],
        compiler_params=pltpu.CompilerParams(
            collective_id=0, has_side_effects=True, vmem_limit_bytes=VMEM_LIMIT
        ),
        name="gather",
    )(block_ids, block_ids, owner_map, slots, offsets, counts, table)


def solve(unobserved, spots, landed, gramian, confidence, counts):
    users = confidence.shape[0]
    return pl.pallas_call(
        functools.partial(solve_kernel, unobserved),
        out_shape=jax.ShapeDtypeStruct((users, LANES), F32),
        in_specs=[smem(), anywhere(), vmem(), vmem(), vmem()],
        out_specs=vmem(),
        scratch_shapes=[
            pltpu.VMEM(landed.shape, BF16),
            pltpu.VMEM(landed.shape, F32),
            pltpu.VMEM((USER_ITEMS * users, LANES), F32),
            pltpu.VMEM((USER_ITEMS, LANES, users), F32),
            pltpu.VMEM((USER_ITEMS, users), F32),
            pltpu.SemaphoreType.DMA((8,)),
        ],
        compiler_params=pltpu.CompilerParams(vmem_limit_bytes=VMEM_LIMIT),
        name="solve",
    )(spots, landed, gramian, confidence, counts)


def fetch_all(shards, gy_size, blocks_dev, item_table, block_ids, item_slots, item_offsets, item_counts, owner_map):
    users = block_ids.shape[0]
    live = jnp.arange(USER_ITEMS)[None, :] < item_counts[:, None]
    row_index = item_slots * BLOCK + item_offsets
    candidates = jnp.arange(USER_BLOCKS * BLOCK, dtype=jnp.int32)
    hits = row_index[:, :, None] == candidates[None, None, :]
    need = jnp.any(hits & live[:, :, None], axis=1).astype(F32)
    asked, keys, _ = ask(
        shards,
        gy_size,
        blocks_dev,
        block_ids.reshape(-1, LANES),
        owner_map,
        need.reshape(users * USER_BLOCKS, BLOCK),
    )
    keys = keys.reshape(users, 1, USER_BLOCKS * BLOCK)
    spots = jnp.sum(jnp.where(hits, keys, 0), axis=2)
    landed, gramian = fetch(shards, gy_size, MOST, asked.reshape(shards, LANES), item_table)
    return spots, landed, gramian


def per_device(item_table, block_ids, item_slots, item_offsets, confidence, item_counts, owner_map):
    shards, gy_size = lax.axis_size(("gx", "gy")), lax.axis_size("gy")
    rows_dev = item_table.shape[0]
    blocks_dev = rows_dev // BLOCK
    users = block_ids.shape[0]
    unobserved = USER_ITEMS / (rows_dev * shards)
    owner_map = owner_map.reshape(-1, LANES)
    counts = item_counts.reshape(1, users)

    def finish(spots, landed, gramian):
        landed = landed.reshape(-1, LANES)
        gramian = gramian.reshape(LANES, LANES)
        return solve(unobserved, spots, landed, gramian, confidence, counts)

    landed, gramian, spots, top = gather(
        shards, gy_size, blocks_dev, block_ids, owner_map,
        item_slots, item_offsets, counts, item_table,
    )
    return lax.cond(
        top[0, 0] >= MARK,
        lambda: finish(
            *fetch_all(
                shards, gy_size, blocks_dev, item_table, block_ids,
                item_slots, item_offsets, item_counts, owner_map,
            )
        ),
        lambda: finish(spots, landed, gramian),
    )


def solution(mesh):
    return jax.shard_map(
        per_device,
        mesh=mesh,
        in_specs=(
            P(("gx", "gy"), None),
            P(("gx", "gy"), None),
            P(("gx", "gy"), None),
            P(("gx", "gy"), None),
            P(("gx", "gy"), None),
            P(("gx", "gy")),
            P(),
        ),
        out_specs=P(("gx", "gy"), None),
        check_vma=False,
    )
```

profile of v0, /device:TPU:1, one launch (start us, length us, event | category | flops | bytes accessed | tf_op | source)
XLA Modules:
  0.0 87.3 jit_solution(2555197270485461138)
XLA Ops:
  0.0 0.0 copy-start.5
  0.0 0.0 copy-start
  0.0 0.0 copy-start.2
  0.0 0.0 copy-start.3
  0.0 0.0 copy-start.6
  0.0 0.0 copy-start.4
  0.0 1.5 %copy.33.ids.id_rows = s32[128,8]{1,0:T(8,128)} copy(s32[128,8]{0,1:T(8,128)} %param.10) | data formatting | bytes 8192 | tf_op args[1]
  1.5 1.4 %copy.35.slots = s32[128,32]{1,0:T(8,128)} copy(s32[128,32]{0,1:T(8,128)} %param.11) | data formatting | bytes 32768 | tf_op args[2]
  3.0 1.4 %copy.36.offsets = s32[128,32]{1,0:T(8,128)} copy(s32[128,32]{0,1:T(8,128)} %param.12) | data formatting | bytes 32768 | tf_op args[3]
  4.4 64.4 %gather.1 = (bf16[128,48,128]{2,1,0:T(8,128)(2,1)S(1)}, f32[128,1,128]{2,1,0:T(1,128)S(1)}, s32[128,32]{1,0:T(8,128)S(1)}, s32[1,1]{1,0:T(1,128)}) custom-call(s32[128,8]{1,0:T(8,128)} %copy.33.ids.id_rows, s32[128,8]{1,0:T(8,128)} %copy.33.ids.id_rows, s32[2048,128]{1,0:T(8,128)} %bitcast.10, s32[128,32]{1,0:T(8,128)} %copy.35.slots, ...), custom_call_target="tpu_custom_call" | custom-call | tf_op jit(solution)/shard_map/gather/pallas_call | solution.py:611
  69.4 0.0 copy-done.5
  69.4 0.0 copy-done
  69.4 0.0 copy-done.2
  69.4 0.0 copy-done.3
  69.4 0.0 copy-done.6
  69.5 0.0 copy-done.4
  69.5 17.2 %conditional.1 = (f32[128,128]{1,0:T(8,128)S(1)}) conditional(s32[]{:T(128)} %bitcast.8, (bf16[128,48,128]{2,1,0:T(8,128)(2,1)S(1)}, f32[128,1,128]{2,1,0:T(1,128)S(1)}, s32[128,32]{1,0:T(8,128)S(1)}, f32[128,32]{0,1:T(8,128)S(1)}, s32[1,128]{1,0:T(1,128)S(1)}) %tuple.30, (s32[128,32]{0,1:T(8,128)S(1)}, s32[128,32]{0,1:T(8,128)S(1)}, ...), branch_computations={%region_0.0_spmd, %region_1.4_spmd} | conditional | flops 1581056 | bytes 533000 | solution.py:705
  69.5 0.7 copy.38.confidence
  70.2 16.3 %solve.2 = f32[128,128]{1,0:T(8,128)S(1)} custom-call(s32[128,32]{1,0:T(8,128)S(1)} %get-tuple-element.34.spots, bf16[6144,128]{1,0:T(8,128)(2,1)S(1)} %bitcast.12, f32[128,128]{1,0:T(8,128)S(1)} %bitcast.15, f32[128,32]{1,0:T(8,128)} %copy.38.confidence, s32[1,128]{1,0:T(1,128)S(1)} %get-tuple-element.38.counts), custom_call_target="tpu_custom_call" | custom-call | tf_op jit(solution)/shard_map/cond/branch_0_fun/solve/pallas_call | solution.py:648
  86.7 0.0 copy-start.1
  86.7 0.6 copy-done.1
Async XLA Ops:
  0.0 69.4 %copy-start.5 = (s32[128,8]{0,1:T(8,128)S(1)}, s32[128,8]{0,1:T(8,128)}, u32[]{:S(2)}) copy-start(s32[128,8]{0,1:T(8,128)} %param.10) | copy-start | bytes 12292
  0.0 69.4 %copy-start = (s32[262144]{0:T(1024)S(1)}, s32[262144]{0:T(1024)}, u32[]{:S(2)}) copy-start(s32[262144]{0:T(1024)} %param.15) | copy-start | bytes 3145732
  0.0 69.4 %copy-start.2 = (s32[128,32]{0,1:T(8,128)S(1)}, s32[128,32]{0,1:T(8,128)}, u32[]{:S(2)}) copy-start(s32[128,32]{0,1:T(8,128)} %param.11) | copy-start | bytes 49156
  0.0 69.4 %copy-start.3 = (s32[128,32]{0,1:T(8,128)S(1)}, s32[128,32]{0,1:T(8,128)}, u32[]{:S(2)}) copy-start(s32[128,32]{0,1:T(8,128)} %param.12) | copy-start | bytes 49156
  0.0 69.4 %copy-start.6 = (s32[128]{0:T(128)S(1)}, s32[128]{0:T(128)}, u32[]{:S(2)}) copy-start(s32[128]{0:T(128)} %param.14) | copy-start | bytes 1540
  0.0 69.4 %copy-start.4 = (f32[128,32]{0,1:T(8,128)S(1)}, f32[128,32]{0,1:T(8,128)}, u32[]{:S(2)}) copy-start(f32[128,32]{0,1:T(8,128)} %param.13) | copy-start | bytes 49156
  86.7 0.6 copy-start.1
where the time goes:
time: 87.7 us; the launch traced here: 87.3 us
  Pallas kernels  80.6 us (92%)
  local copies, waits for them, and re-layouts  5.75 us (7%)
    pallas_call x1, Pallas kernels, gather(): pl.pallas_call(functools.partial(gather_kernel, shards, gy_size, blocks_d...  64.4 us
    pallas_call x1, Pallas kernels, solve(): pl.pallas_call(functools.partial(solve_kernel, unobserved), out_shape=jax...  16.3 us
    unnamed x17, local copies, waits for them, and re-layouts  5.02 us

commit v1 on v0

--- a/solution.py
+++ b/solution.py
@@ -19,6 +19,8 @@
 MOST = 128
 MARK = 1 << 20
 
+SECOND = 64
+
 MESH = pl.DeviceIdType.MESH
 F32 = jnp.float32
 BF16 = jnp.bfloat16
@@ -53,7 +55,7 @@
         dst_ref=dst,
         send_sem=send_sem,
         recv_sem=recv_sem,
-        device_id=(peer // gy_size, lax.rem(peer, gy_size)),
+        device_id=peer if isinstance(peer, tuple) else (peer // gy_size, lax.rem(peer, gy_size)),
         device_id_type=MESH,
     )
 
@@ -237,21 +239,23 @@
     return (gx // CORES) * gy_size + gy, lax.rem(gx, CORES)
 
 
-def shifted(me, off, gy_size):
+def shift_from(me, gy_size):
     gx, gy = me // gy_size, lax.rem(me, gy_size)
     y, core, x, z = gx // CORES, lax.rem(gx, CORES), gy // RING, lax.rem(gy, RING)
-    z = lax.rem(z + lax.rem(off, RING), RING)
-    x = lax.rem(x + lax.rem(off // RING, RING), RING)
-    core = lax.rem(core + lax.rem(off // (RING * RING), CORES), CORES)
-    y = lax.rem(y + off // (RING * RING * CORES), RING)
-    return (y * CORES + core) * gy_size + x * RING + z
+
+    def shifted(off):
+        gx = lax.rem(y + off // (RING * RING * CORES), RING) * CORES
+        gx = gx + lax.rem(core + off // (RING * RING), CORES)
+        return gx, lax.rem(x + off // RING, RING) * RING + lax.rem(z + off, RING)
+
+    return shifted
 
 
 def gather_kernel(
     shards, gy_size, blocks_dev, ids, id_rows, owner_map, slots, offsets, counts, table,
     landed, gramian, spots, top,
     owners, found, queries, asked, asked_here, packed, twin_packed, wide, stage, outgoing,
-    terms, arrived, row_total, load_sem, own_sem, table_send, table_recv,
+    terms, arrived, row_total, spreads, starts, chips, load_sem, own_sem, table_send, table_recv,
     send_sem, recv_sem, ask_send, ask_recv, term_send, term_recv, sum_send, sum_recv,
 ):
     me = place(gy_size)
@@ -270,7 +274,7 @@
     for c in range(parts):
         load(c).start()
 
-    users = slots.shape[0]
+    users = slots.shape[1]
     requests = found.shape[0]
     group = LANES // USER_BLOCKS
     lane = lax.broadcasted_iota(jnp.int32, (LANES, LANES), 1)
@@ -278,32 +282,34 @@
     lane_f = lane.astype(F32)
     diagonal = lane == sub
 
-    count = jnp.sum(jnp.where(diagonal, counts[...], 0).astype(F32), axis=1, keepdims=True)
+    item_sub = lax.broadcasted_iota(jnp.int32, (USER_ITEMS, users), 0)
     slot_lane = lax.broadcasted_iota(jnp.int32, (users, USER_ITEMS), 1)
     row_index = slots[...] * BLOCK + offsets[...]
-    row_index = jnp.where(slot_lane < count.astype(jnp.int32), row_index, -1)
+    row_index = jnp.where(item_sub < counts[...], row_index, -1).astype(F32)
+    inner = (id_rows[...] & (LANES - 1)).astype(F32)
+    by_user = jnp.concatenate(
+        [row_index, inner, jnp.zeros((LANES - USER_ITEMS - USER_BLOCKS, users), F32)], axis=0
+    ).T
+    row_index = by_user[:, :USER_ITEMS].astype(jnp.int32)
+    inner = by_user.astype(BF16)
     wanted = lane == row_index[:, 0:1]
     for item in range(1, USER_ITEMS):
         wanted = wanted | (lane == row_index[:, item : item + 1])
     wanted = jnp.where(wanted, 1.0, 0.0).astype(BF16)
-    inner = jnp.zeros((users, LANES), F32)
-    for slot in range(USER_BLOCKS):
-        id_low = (id_rows[:, slot : slot + 1] & (LANES - 1)).astype(F32)
-        inner = jnp.where(lane == slot, id_low, inner)
-    inner = inner.astype(BF16)
+    wanted_inner = jnp.concatenate([wanted, inner], axis=1)
 
     load_map.wait()
 
     def look(user, carry):
         for slot in range(USER_BLOCKS):
-            line = lax.shift_right_logical(ids[user, slot], bits(LANES))
+            line = lax.shift_right_logical(ids[slot, user], bits(LANES))
             found[pl.ds(user * USER_BLOCKS + slot, 1), :] = owners[pl.ds(line, 1), :]
         return carry
 
     lax.fori_loop(0, users, look, 0, unroll=2)
 
     same = lax.shift_right_logical(lane, 3) == (sub & 7)
-    own_lane = lane == (sub & 7)
+    own_lane = lane == (sub & 7) + USER_ITEMS
     earlier = jnp.where(lane < sub, 1.0, 0.0).astype(BF16)
     before_row = jnp.where(
         (lax.shift_right_logical(lane, 3) == lax.shift_right_logical(sub, 3))
@@ -311,19 +317,16 @@
         1.0,
         0.0,
     ).astype(BF16)
-    up_to = [jnp.where((sub & 7) <= r, 1.0, 0.0).astype(BF16) for r in range(BLOCK)]
+    up_to = jnp.concatenate(
+        [jnp.where((sub & 7) <= r, 1.0, 0.0).astype(BF16) for r in range(BLOCK)], axis=1
+    )
     total = jnp.zeros((1, LANES), F32)
     low_high = jnp.zeros((LANES, 2 * LANES), F32)
-    pos_chip = jnp.zeros((users, 2 * LANES), F32)
     for a in range(requests // LANES):
-        pick = jnp.where(sub // USER_BLOCKS + a * group == lane, 1.0, 0.0).astype(BF16)
-        place_back = jnp.where(lane // USER_BLOCKS + a * group == sub, 1.0, 0.0).astype(BF16)
-        spread = jnp.dot(pick, wanted, preferred_element_type=F32)
-        spread = jnp.where(same, spread, 0.0)
-        live = spread > 0.0
-        spread = spread.astype(BF16)
-        inner_here = jnp.dot(pick, inner, preferred_element_type=F32)
-        inner_here = jnp.sum(jnp.where(own_lane, inner_here, 0.0), axis=1, keepdims=True)
+        pick = jnp.where(lax.shift_right_logical(sub, bits(USER_BLOCKS)) + a * group == lane, 1.0, 0.0).astype(BF16)
+        picked = jnp.dot(pick, wanted_inner, preferred_element_type=F32)
+        spread = jnp.where(same, picked[:, :LANES], 0.0).astype(BF16)
+        inner_here = jnp.sum(jnp.where(own_lane, picked[:, LANES:], 0.0), axis=1, keepdims=True)
         line = found[pl.ds(a * LANES, LANES), :].astype(F32)
         storage = jnp.sum(jnp.where(lane_f == inner_here, line, 0.0), axis=1, keepdims=True)
         storage = storage.astype(jnp.int32)
@@ -335,7 +338,8 @@
         low_first = ((within & 15) * BLOCK).astype(F32)
         high = (core * (rows_dev // LANES) + lax.shift_right_logical(within, 4)).astype(F32)
         chip = chip.astype(F32)
-        so_far = [jnp.dot(spread, m, preferred_element_type=F32) for m in up_to]
+        so_far = jnp.dot(spread, up_to, preferred_element_type=F32)
+        so_far = [so_far[:, r * LANES : (r + 1) * LANES] for r in range(BLOCK)]
         mine = lane_f == chip
         counted = jnp.where(mine, so_far[-1], 0.0)
         before = jnp.dot(earlier, counted.astype(BF16), preferred_element_type=F32) + total
@@ -352,47 +356,49 @@
         chip_row = jnp.sum(jnp.where(diagonal, chip, 0.0), axis=0, keepdims=True)
         to_chip = jnp.where(sub.astype(F32) == chip_row, 1.0, 0.0).astype(BF16)
         low_high = low_high + jnp.dot(to_chip, both, preferred_element_type=F32)
-        spot = jnp.dot(spread, before_row, preferred_element_type=F32) + start
-        both = jnp.concatenate(
-            [jnp.where(live, spot, 0.0), jnp.where(live, chip, 0.0)], axis=1
-        ).astype(BF16)
-        pos_chip = pos_chip + jnp.dot(place_back, both, preferred_element_type=F32)
+        here = pl.ds(a * LANES, LANES)
+        spreads[here, :] = spread
+        starts[here, :] = jnp.broadcast_to(start, (LANES, LANES))
+        chips[here, :] = jnp.broadcast_to(chip, (LANES, LANES))
     most = jnp.max(total, axis=1, keepdims=True)
     mark = jnp.where(most > CHIP_ROOM, float(MARK), 0.0)
     query = (low_high[:, :LANES] + low_high[:, LANES:] * float(LANES) + mark).astype(jnp.int32)
-    for o in range(shards // CORES):
-        queries[o] = query[o : o + 1, :]
-
-    pl.semaphore_wait(barrier, shards - 1)
-    twin = shifted(me, RING * RING, gy_size)
-    lend = send(table, twin_packed, table_send, table_recv, twin, gy_size)
-    lend.start()
-
-    def ask_one(i, carry):
-        peer = lax.rem(me + i, shards)
-        chip, _ = chip_of(peer, gy_size)
-        send(queries.at[chip], asked.at[me], ask_send, ask_recv, peer, gy_size).start()
-        return carry
-
-    lax.fori_loop(1, shards, ask_one, 0)
-    own_ask = pltpu.make_async_copy(queries.at[chip_me], asked.at[me], own_sem.at[1])
-    own_ask.start()
-
-    piece = min(512, part)
-    gram = jnp.zeros((LANES, LANES), F32)
+    for core in range(CORES):
+        shares = pltpu.roll(query, LANES - core * ROOM, 1) if core else query
+        for o in range(shards // CORES):
+            device = (o // gy_size * CORES + core) * gy_size + o % gy_size
+            queries[device] = shares[o : o + 1, :]
+
+    piece = min(512, rows_dev)
     mine_from = core_me * rows_dev
+    theirs_from = (CORES - 1 - core_me) * rows_dev
+
+    def widen(source, start, j, carry):
+        at = j * piece
+        block = source[pl.ds(pl.multiple_of(at, piece), piece), :]
+        wide[pl.ds(pl.multiple_of(start + at, piece), piece), :] = block.astype(F32)
+        return carry
+
     for c in range(parts):
         load(c).wait()
-
-        def step(j, gram):
-            at = c * part + j * piece
-            block = packed[pl.ds(pl.multiple_of(at, piece), piece), :]
-            wide[pl.ds(pl.multiple_of(mine_from + at, piece), piece), :] = block.astype(F32)
-            return gram + lax.dot_general(
-                block, block, (((0,), (0,)), ((), ())), preferred_element_type=F32
-            )
-
-        gram = lax.fori_loop(0, part // piece, step, gram)
+    lax.fori_loop(0, rows_dev // piece, functools.partial(widen, packed, mine_from), 0)
+
+    pl.semaphore_wait(barrier, shards - 1)
+    shifted = shift_from(me, gy_size)
+    twin = shifted(RING * RING)
+    lend = send(table, twin_packed, table_send, table_recv, twin, gy_size)
+    exchange_rows(queries, asked, me, shards, gy_size, ask_send, ask_recv)
+    lend.start()
+    own_ask = pltpu.make_async_copy(queries.at[me], asked.at[me], own_sem.at[1])
+    own_ask.start()
+
+    def step(j, gram):
+        block = packed[pl.ds(pl.multiple_of(j * piece, piece), piece), :]
+        return gram + lax.dot_general(
+            block, block, (((0,), (0,)), ((), ())), preferred_element_type=F32
+        )
+
+    gram = lax.fori_loop(0, rows_dev // piece, step, jnp.zeros((LANES, LANES), F32))
     for o in range(LANES):
         terms[o] = gram[o : o + 1, :]
     exchange_rows(terms, arrived, me, shards, gy_size, term_send, term_recv)
@@ -404,33 +410,25 @@
     to_scalars = pltpu.make_async_copy(asked, asked_here, own_sem.at[3])
     to_scalars.start()
     lend.wait()
-    theirs_from = (CORES - 1 - core_me) * rows_dev
-
-    def widen(j, carry):
-        at = j * piece
-        block = twin_packed[pl.ds(pl.multiple_of(at, piece), piece), :]
-        wide[pl.ds(pl.multiple_of(theirs_from + at, piece), piece), :] = block.astype(F32)
-        return carry
-
-    lax.fori_loop(0, rows_dev // piece, widen, 0)
+    lax.fori_loop(0, rows_dev // piece, functools.partial(widen, twin_packed, theirs_from), 0)
     to_scalars.wait()
 
-    my_part = core_me * ROOM
     my_place = chip_me * CORES + core_me
 
     def collect(peer):
         for t in range(ROOM):
-            row = asked_here[peer, 0, my_part + t] & (CORES * rows_dev - 1)
+            row = asked_here[peer, 0, t] & (CORES * rows_dev - 1)
             stage[pl.ds(t, 1), :] = wide[pl.ds(row, 1), :]
         outgoing[peer] = stage[...].astype(BF16)
 
     def serve(i, carry):
-        peer = shifted(me, lax.rem(i * 37, shards), gy_size)
+        gx, gy = shifted(lax.rem(i * 37, shards))
+        peer = gx * gy_size + gy
         collect(peer)
-        send(outgoing.at[peer], landed.at[my_place], send_sem, recv_sem, peer, gy_size).start()
-        return carry
-
-    lax.fori_loop(1, shards // 2, serve, 0)
+        send(outgoing.at[peer], landed.at[my_place], send_sem, recv_sem, (gx, gy), gy_size).start()
+        return carry
+
+    lax.fori_loop(1, SECOND, serve, 0)
     own_term.wait()
     await_rows(terms, arrived, shards, gy_size, term_send, term_recv)
     row_total[...] = jnp.sum(arrived[...], axis=0)
@@ -443,11 +441,23 @@
     lax.fori_loop(1, shards, share, 0)
     own_sum = pltpu.make_async_copy(row_total, gramian.at[me], own_sem.at[4])
     own_sum.start()
-    lax.fori_loop(shards // 2, shards, serve, 0)
+    lax.fori_loop(SECOND, shards, serve, 0)
     collect(me)
     own = pltpu.make_async_copy(outgoing.at[me], landed.at[my_place], own_sem.at[5])
     own.start()
 
+    pos_chip = jnp.zeros((users, 2 * LANES), F32)
+    for a in range(requests // LANES):
+        here = pl.ds(a * LANES, LANES)
+        back = lax.shift_right_logical(lane, bits(USER_BLOCKS)) + a * group == sub
+        spread = spreads[here, :]
+        live = spread.astype(F32) > 0.0
+        spot = jnp.dot(spread, before_row, preferred_element_type=F32) + starts[here, :]
+        both = jnp.concatenate(
+            [jnp.where(live, spot, 0.0), jnp.where(live, chips[here, :], 0.0)], axis=1
+        ).astype(BF16)
+        back = jnp.where(back, 1.0, 0.0).astype(BF16)
+        pos_chip = pos_chip + jnp.dot(back, both, preferred_element_type=F32)
     spot = pos_chip[:, :LANES] + pos_chip[:, LANES:] * float(CHIP_ROOM)
     spots_now = jnp.zeros((users, USER_ITEMS), F32)
     for item in range(USER_ITEMS):
@@ -466,7 +476,7 @@
 def solve_kernel(
     unobserved, spots, landed, gramian, confidence, counts, out, packed, wide, rows, vectors, weights, sem
 ):
-    users = confidence.shape[0]
+    users = confidence.shape[1]
     parts = 8
     part = landed.shape[0] // parts
 
@@ -500,7 +510,7 @@
         )
 
     item_sub = lax.broadcasted_iota(jnp.int32, (USER_ITEMS, users), 0)
-    weights[...] = jnp.where(item_sub < counts[...], confidence[...].T, 0.0)
+    weights[...] = jnp.where(item_sub < counts[...], confidence[...], 0.0)
     scaled = gramian[...] * unobserved
     top = scaled.astype(BF16)
     rest = (scaled - top.astype(F32)).astype(BF16)
@@ -606,7 +616,7 @@
 
 def gather(shards, gy_size, blocks_dev, block_ids, owner_map, slots, offsets, counts, table):
     dma = pltpu.SemaphoreType.DMA
-    users = slots.shape[0]
+    users = slots.shape[1]
     line = (shards, 1, LANES)
     return pl.pallas_call(
         functools.partial(gather_kernel, shards, gy_size, blocks_dev),
@@ -621,7 +631,7 @@
         scratch_shapes=[
             pltpu.VMEM(owner_map.shape, jnp.int32),
             pltpu.VMEM((users * USER_BLOCKS, LANES), jnp.int32),
-            pltpu.VMEM((shards // CORES, 1, LANES), jnp.int32),
+            pltpu.VMEM(line, jnp.int32),
             pltpu.VMEM(line, jnp.int32),
             pltpu.SMEM(line, jnp.int32),
             pltpu.VMEM(table.shape, BF16),
@@ -632,6 +642,9 @@
             pltpu.VMEM(line, F32),
             pltpu.VMEM(line, F32),
             pltpu.VMEM((1, LANES), F32),
+            pltpu.VMEM((users * USER_BLOCKS, LANES), BF16),
+            pltpu.VMEM((users * USER_BLOCKS, LANES), F32),
+            pltpu.VMEM((users * USER_BLOCKS, LANES), F32),
             pltpu.SemaphoreType.DMA((8,)),
             pltpu.SemaphoreType.DMA((6,)),
             dma, dma, dma, dma, dma, dma, dma, dma, dma, dma,
@@ -644,7 +657,7 @@
 
 
 def solve(unobserved, spots, landed, gramian, confidence, counts):
-    users = confidence.shape[0]
+    users = confidence.shape[1]
     return pl.pallas_call(
         functools.partial(solve_kernel, unobserved),
         out_shape=jax.ShapeDtypeStruct((users, LANES), F32),
@@ -696,11 +709,11 @@
     def finish(spots, landed, gramian):
         landed = landed.reshape(-1, LANES)
         gramian = gramian.reshape(LANES, LANES)
-        return solve(unobserved, spots, landed, gramian, confidence, counts)
+        return solve(unobserved, spots, landed, gramian, confidence.T, counts)
 
     landed, gramian, spots, top = gather(
-        shards, gy_size, blocks_dev, block_ids, owner_map,
-        item_slots, item_offsets, counts, item_table,
+        shards, gy_size, blocks_dev, block_ids.T, owner_map,
+        item_slots.T, item_offsets.T, counts, item_table,
     )
     return lax.cond(
         top[0, 0] >= MARK,

time: 87.7 us -> 72.8 us (0.83)
  Pallas kernels: 80.6 us -> 71.1 us
  local copies, waits for them, and re-layouts: 5.75 us -> 0.65 us
    pallas_call x1, Pallas kernels: 64.4 us -> 54.9 us  [gather(): pl.pallas_call(functools.partial(gather_kernel, shards, gy_size, blocks_d...]
    unnamed x17 -> x14, local copies, waits for them, and re-layouts: 5.02 us -> 0.65 us
where the time goes in v1:
time: 72.8 us; the launch traced here: 72.7 us
  Pallas kernels  71.1 us (98%)
    pallas_call x1, Pallas kernels, gather(): pl.pallas_call(functools.partial(gather_kernel, shards, gy_size, blocks_d...  54.9 us
    pallas_call x1, Pallas kernels, solve(): pl.pallas_call(functools.partial(solve_kernel, unobserved), out_shape=jax...  16.3 us

profile of v1, /device:TPU:1, one launch (start us, length us, event | category | flops | bytes accessed | tf_op | source)
XLA Modules:
  0.0 72.7 jit_solution(11255225371191422673)
XLA Ops:
  0.0 0.0 copy-start.6
  0.0 0.0 copy-start.1
  0.0 0.0 copy-start.3
  0.0 0.0 copy-start.2
  0.0 0.0 copy-start.5
  0.0 0.0 copy-start
  0.0 54.9 %gather.1 = (bf16[128,48,128]{2,1,0:T(8,128)(2,1)S(1)}, f32[128,1,128]{2,1,0:T(1,128)S(1)}, s32[128,32]{1,0:T(8,128)S(1)}, s32[1,1]{1,0:T(1,128)}) custom-call(s32[8,128]{1,0:T(8,128)} %bitcast.25, s32[8,128]{1,0:T(8,128)} %bitcast.26, s32[2048,128]{1,0:T(8,128)} %bitcast.15, s32[32,128]{1,0:T(8,128)} %bitcast.22, s32[32,128]{1,0:T(8,128)} %bitcast.23, ...), custom_call_target="tpu_custom_call" | custom-call | tf_op jit(solution)/shard_map/gather/pallas_call | solution.py:621
  55.5 0.0 copy-done.6
  55.5 0.0 copy-done.1
  55.5 0.0 copy-done.3
  55.5 0.0 copy-done.2
  55.5 0.0 copy-done.5
  55.5 0.0 copy-done
  55.5 16.5 %conditional.1 = (f32[128,128]{1,0:T(8,128)S(1)}) conditional(s32[]{:T(128)} %bitcast.13, (bf16[128,48,128]{2,1,0:T(8,128)(2,1)S(1)}, f32[128,1,128]{2,1,0:T(1,128)S(1)}, f32[128,32]{0,1:T(8,128)S(1)}, s32[128,32]{1,0:T(8,128)S(1)}, s32[1,128]{1,0:T(1,128)S(1)}) %tuple.30, (s32[128,32]{0,1:T(8,128)S(1)}, s32[128,32]{0,1:T(8,128)S(1)}, ...), branch_computations={%region_0.0_spmd, %region_1.4_spmd} | conditional | flops 1581056 | bytes 500232 | solution.py:718
  55.5 16.3 %solve.2 = f32[128,128]{1,0:T(8,128)S(1)} custom-call(s32[128,32]{1,0:T(8,128)S(1)} %get-tuple-element.34.spots, bf16[6144,128]{1,0:T(8,128)(2,1)S(1)} %bitcast.17, f32[128,128]{1,0:T(8,128)S(1)} %bitcast.24, f32[32,128]{1,0:T(8,128)S(1)} %bitcast.20, s32[1,128]{1,0:T(1,128)S(1)} %get-tuple-element.38.counts), custom_call_target="tpu_custom_call" | custom-call | tf_op jit(solution)/shard_map/cond/branch_0_fun/solve/pallas_call | solution.py:661
  72.0 0.0 copy-start.4
  72.1 0.6 copy-done.4
Async XLA Ops:
  0.0 55.5 %copy-start.6 = (s32[128]{0:T(128)S(1)}, s32[128]{0:T(128)}, u32[]{:S(2)}) copy-start(s32[128]{0:T(128)} %param.14) | copy-start | bytes 1540
  0.0 55.5 %copy-start.1 = (f32[128,32]{0,1:T(8,128)S(1)}, f32[128,32]{0,1:T(8,128)}, u32[]{:S(2)}) copy-start(f32[128,32]{0,1:T(8,128)} %param.13) | copy-start | bytes 49156
  0.0 55.5 %copy-start.3 = (s32[128,32]{0,1:T(8,128)S(1)}, s32[128,32]{0,1:T(8,128)}, u32[]{:S(2)}) copy-start(s32[128,32]{0,1:T(8,128)} %param.12) | copy-start | bytes 49156
  0.0 55.5 %copy-start.2 = (s32[128,32]{0,1:T(8,128)S(1)}, s32[128,32]{0,1:T(8,128)}, u32[]{:S(2)}) copy-start(s32[128,32]{0,1:T(8,128)} %param.11) | copy-start | bytes 49156
  0.0 55.5 %copy-start.5 = (s32[128,8]{0,1:T(8,128)S(1)}, s32[128,8]{0,1:T(8,128)}, u32[]{:S(2)}) copy-start(s32[128,8]{0,1:T(8,128)} %param.10) | copy-start | bytes 12292
  0.0 55.5 %copy-start = (s32[262144]{0:T(1024)S(1)}, s32[262144]{0:T(1024)}, u32[]{:S(2)}) copy-start(s32[262144]{0:T(1024)} %param.15) | copy-start | bytes 3145732
  72.0 0.6 copy-start.4

commit v2 on v1

--- a/solution.py
+++ b/solution.py
@@ -200,7 +200,7 @@
         outgoing[peer] = stage[...].astype(BF16)
 
     def serve(i, carry):
-        off = lax.rem(i * 37, shards)
+        off = lax.rem(i * 77, shards)
         peer = lax.rem(me + off, shards)
         collect(peer)
         send(outgoing.at[peer], landed.at[me], send_sem, recv_sem, peer, gy_size).start()
@@ -251,11 +251,63 @@
     return shifted
 
 
+def conjugate(unobserved, gramian, confidence, counts, out, rows, vectors, weights):
+    users = confidence.shape[1]
+    unit = jnp.where(
+        lax.broadcasted_iota(jnp.int32, (LANES, LANES), 0)
+        == lax.broadcasted_iota(jnp.int32, (LANES, LANES), 1),
+        1.0,
+        0.0,
+    ).astype(BF16)
+    for item in range(USER_ITEMS):
+        block = rows[pl.ds(item * users, users), :].astype(BF16)
+        vectors[item] = lax.dot_general(
+            unit, block, (((1,), (1,)), ((), ())), preferred_element_type=F32
+        )
+
+    item_sub = lax.broadcasted_iota(jnp.int32, (USER_ITEMS, users), 0)
+    weights[...] = jnp.where(item_sub < counts[...], confidence[...], 0.0)
+    scaled = gramian * unobserved
+    top = scaled.astype(BF16)
+    rest = (scaled - top.astype(F32)).astype(BF16)
+
+    right = jnp.zeros((LANES, users), F32)
+    for item in range(USER_ITEMS):
+        right = right + vectors[item] * weights[item : item + 1, :]
+    norm = jnp.sum(right * right, axis=0, keepdims=True)
+
+    def sweep(_, carry):
+        solution, residual, direction, norm = carry
+        d_top = direction.astype(BF16)
+        d_rest = (direction - d_top.astype(F32)).astype(BF16)
+        image = direction + (
+            jnp.dot(top, d_top, preferred_element_type=F32)
+            + jnp.dot(top, d_rest, preferred_element_type=F32)
+            + jnp.dot(rest, d_top, preferred_element_type=F32)
+        )
+        for item in range(USER_ITEMS):
+            vector = vectors[item]
+            projected = jnp.sum(vector * direction, axis=0, keepdims=True)
+            image = image + vector * (weights[item : item + 1, :] * projected)
+        alpha = norm / jnp.sum(direction * image, axis=0, keepdims=True)
+        solution = solution + alpha * direction
+        residual = residual - alpha * image
+        after = jnp.sum(residual * residual, axis=0, keepdims=True)
+        direction = residual + (after / norm) * direction
+        return solution, residual, direction, after
+
+    solution, *_ = lax.fori_loop(
+        0, ITERATIONS, sweep, (jnp.zeros_like(right), right, right, norm)
+    )
+    out[...] = solution.T
+
+
 def gather_kernel(
-    shards, gy_size, blocks_dev, ids, id_rows, owner_map, slots, offsets, counts, table,
-    landed, gramian, spots, top,
+    shards, gy_size, blocks_dev, unobserved,
+    ids, id_rows, owner_map, slots, offsets, counts, confidence, table, out, top,
     owners, found, queries, asked, asked_here, packed, twin_packed, wide, stage, outgoing,
-    terms, arrived, row_total, spreads, starts, chips, load_sem, own_sem, table_send, table_recv,
+    terms, arrived, row_total, spreads, starts, chips,
+    landed, gramian, spots, spots_here, rows, vectors, weights, load_sem, own_sem, table_send, table_recv,
     send_sem, recv_sem, ask_send, ask_recv, term_send, term_recv, sum_send, sum_recv,
 ):
     me = place(gy_size)
@@ -392,13 +444,15 @@
     own_ask = pltpu.make_async_copy(queries.at[me], asked.at[me], own_sem.at[1])
     own_ask.start()
 
+    slab = min(2048, rows_dev)
+
     def step(j, gram):
-        block = packed[pl.ds(pl.multiple_of(j * piece, piece), piece), :]
+        block = packed[pl.ds(pl.multiple_of(j * slab, slab), slab), :]
         return gram + lax.dot_general(
             block, block, (((0,), (0,)), ((), ())), preferred_element_type=F32
         )
 
-    gram = lax.fori_loop(0, rows_dev // piece, step, jnp.zeros((LANES, LANES), F32))
+    gram = lax.fori_loop(0, rows_dev // slab, step, jnp.zeros((LANES, LANES), F32))
     for o in range(LANES):
         terms[o] = gram[o : o + 1, :]
     exchange_rows(terms, arrived, me, shards, gy_size, term_send, term_recv)
@@ -422,7 +476,7 @@
         outgoing[peer] = stage[...].astype(BF16)
 
     def serve(i, carry):
-        gx, gy = shifted(lax.rem(i * 37, shards))
+        gx, gy = shifted(lax.rem(i * 77, shards))
         peer = gx * gy_size + gy
         collect(peer)
         send(outgoing.at[peer], landed.at[my_place], send_sem, recv_sem, (gx, gy), gy_size).start()
@@ -467,10 +521,32 @@
     spots[...] = spots_now.astype(jnp.int32)
     top[...] = jnp.max(jnp.max(asked[...], axis=0), axis=1, keepdims=True)
 
+    spots_to = pltpu.make_async_copy(spots, spots_here, own_sem.at[0])
+    spots_to.start()
+
     own_sum.wait()
     own.wait()
     await_rows(terms, gramian, shards, gy_size, sum_send, sum_recv)
+    spots_to.wait()
     await_rows(outgoing, landed, shards, gy_size, send_sem, recv_sem)
+
+    def widen_landed(j, carry):
+        for t in range(8):
+            at = pl.ds(pl.multiple_of((j * 8 + t) * ROOM, ROOM), ROOM)
+            wide[at, :] = landed[j * 8 + t].astype(F32)
+        return carry
+
+    lax.fori_loop(0, shards // 8, widen_landed, 0)
+
+    def take(user, carry):
+        for item in range(USER_ITEMS):
+            spot = spots_here[user, item] & (CORES * rows_dev - 1)
+            rows[pl.ds(item * users + user, 1), :] = wide[pl.ds(spot, 1), :]
+        return carry
+
+    lax.fori_loop(0, users, take, 0)
+    whole = jnp.concatenate([gramian[o] for o in range(LANES)], axis=0)
+    conjugate(unobserved, whole, confidence, counts, out, rows, vectors, weights)
 
 
 def solve_kernel(
@@ -497,53 +573,7 @@
         return carry
 
     lax.fori_loop(0, users, pick, 0)
-    unit = jnp.where(
-        lax.broadcasted_iota(jnp.int32, (LANES, LANES), 0)
-        == lax.broadcasted_iota(jnp.int32, (LANES, LANES), 1),
-        1.0,
-        0.0,
-    ).astype(BF16)
-    for item in range(USER_ITEMS):
-        block = rows[pl.ds(item * users, users), :].astype(BF16)
-        vectors[item] = lax.dot_general(
-            unit, block, (((1,), (1,)), ((), ())), preferred_element_type=F32
-        )
-
-    item_sub = lax.broadcasted_iota(jnp.int32, (USER_ITEMS, users), 0)
-    weights[...] = jnp.where(item_sub < counts[...], confidence[...], 0.0)
-    scaled = gramian[...] * unobserved
-    top = scaled.astype(BF16)
-    rest = (scaled - top.astype(F32)).astype(BF16)
-
-    right = jnp.zeros((LANES, users), F32)
-    for item in range(USER_ITEMS):
-        right = right + vectors[item] * weights[item : item + 1, :]
-    norm = jnp.sum(right * right, axis=0, keepdims=True)
-
-    def sweep(_, carry):
-        solution, residual, direction, norm = carry
-        d_top = direction.astype(BF16)
-        d_rest = (direction - d_top.astype(F32)).astype(BF16)
-        image = direction + (
-            jnp.dot(top, d_top, preferred_element_type=F32)
-            + jnp.dot(top, d_rest, preferred_element_type=F32)
-            + jnp.dot(rest, d_top, preferred_element_type=F32)
-        )
-        for item in range(USER_ITEMS):
-            vector = vectors[item]
-            projected = jnp.sum(vector * direction, axis=0, keepdims=True)
-            image = image + vector * (weights[item : item + 1, :] * projected)
-        alpha = norm / jnp.sum(direction * image, axis=0, keepdims=True)
-        solution = solution + alpha * direction
-        residual = residual - alpha * image
-        after = jnp.sum(residual * residual, axis=0, keepdims=True)
-        direction = residual + (after / norm) * direction
-        return solution, residual, direction, after
-
-    solution, *_ = lax.fori_loop(
-        0, ITERATIONS, sweep, (jnp.zeros_like(right), right, right, norm)
-    )
-    out[...] = solution.T
+    conjugate(unobserved, gramian[...], confidence, counts, out, rows, vectors, weights)
 
 
 def vmem():
@@ -614,20 +644,20 @@
     )(asked, table)
 
 
-def gather(shards, gy_size, blocks_dev, block_ids, owner_map, slots, offsets, counts, table):
+def gather(
+    shards, gy_size, blocks_dev, unobserved, block_ids, owner_map, slots, offsets, counts, confidence, table
+):
     dma = pltpu.SemaphoreType.DMA
     users = slots.shape[1]
     line = (shards, 1, LANES)
     return pl.pallas_call(
-        functools.partial(gather_kernel, shards, gy_size, blocks_dev),
+        functools.partial(gather_kernel, shards, gy_size, blocks_dev, unobserved),
         out_shape=(
-            jax.ShapeDtypeStruct((shards, ROOM, LANES), BF16),
-            jax.ShapeDtypeStruct(line, F32),
-            jax.ShapeDtypeStruct((users, USER_ITEMS), jnp.int32),
+            jax.ShapeDtypeStruct((users, LANES), F32),
             jax.ShapeDtypeStruct((1, 1), jnp.int32),
         ),
-        in_specs=[smem(), vmem(), anywhere(), vmem(), vmem(), vmem(), anywhere()],
-        out_specs=(anywhere(), vmem(), vmem(), vmem()),
+        in_specs=[smem(), vmem(), anywhere(), vmem(), vmem(), vmem(), vmem(), anywhere()],
+        out_specs=(vmem(), vmem()),
         scratch_shapes=[
             pltpu.VMEM(owner_map.shape, jnp.int32),
             pltpu.VMEM((users * USER_BLOCKS, LANES), jnp.int32),
@@ -645,6 +675,13 @@
             pltpu.VMEM((users * USER_BLOCKS, LANES), BF16),
             pltpu.VMEM((users * USER_BLOCKS, LANES), F32),
             pltpu.VMEM((users * USER_BLOCKS, LANES), F32),
+            pltpu.VMEM((shards, ROOM, LANES), BF16),
+            pltpu.VMEM(line, F32),
+            pltpu.VMEM((users, USER_ITEMS), jnp.int32),
+            pltpu.SMEM((users, USER_ITEMS), jnp.int32),
+            pltpu.VMEM((USER_ITEMS * users, LANES), F32),
+            pltpu.VMEM((USER_ITEMS, LANES, users), F32),
+            pltpu.VMEM((USER_ITEMS, users), F32),
             pltpu.SemaphoreType.DMA((8,)),
             pltpu.SemaphoreType.DMA((6,)),
             dma, dma, dma, dma, dma, dma, dma, dma, dma, dma,
@@ -653,7 +690,7 @@
             collective_id=0, has_side_effects=True, vmem_limit_bytes=VMEM_LIMIT
         ),
         name="gather",
-    )(block_ids, block_ids, owner_map, slots, offsets, counts, table)
+    )(block_ids, block_ids, owner_map, slots, offsets, counts, confidence, table)
 
 
 def solve(unobserved, spots, landed, gramian, confidence, counts):
@@ -711,9 +748,9 @@
         gramian = gramian.reshape(LANES, LANES)
         return solve(unobserved, spots, landed, gramian, confidence.T, counts)
 
-    landed, gramian, spots, top = gather(
-        shards, gy_size, blocks_dev, block_ids.T, owner_map,
-        item_slots.T, item_offsets.T, counts, item_table,
+    factors, top = gather(
+        shards, gy_size, blocks_dev, unobserved, block_ids.T, owner_map,
+        item_slots.T, item_offsets.T, counts, confidence.T, item_table,
     )
     return lax.cond(
         top[0, 0] >= MARK,
@@ -723,7 +760,7 @@
                 item_slots, item_offsets, item_counts, owner_map,
             )
         ),
-        lambda: finish(spots, landed, gramian),
+        lambda: factors,
     )
 
 

time: 72.8 us -> 66.2 us (0.909)
  Pallas kernels: 71.1 us -> 64.5 us
    pallas_call x1 -> x0, Pallas kernels: 16.3 us -> none  [solve(): pl.pallas_call(functools.partial(solve_kernel, unobserved), out_shape=jax...]
    pallas_call x1, Pallas kernels: 54.9 us -> 64.5 us  [gather(): pl.pallas_call(functools.partial(gather_kernel, shards, gy_size, blocks_d...]
where the time goes in v2:
time: 66.2 us; the launch traced here: 66 us
  Pallas kernels  64.5 us (97%)
    pallas_call x1, Pallas kernels, gather(): pl.pallas_call(functools.partial(gather_kernel, shards, gy_size, blocks_d...  64.5 us

profile of v2, /device:TPU:1, one launch (start us, length us, event | category | flops | bytes accessed | tf_op | source)
XLA Modules:
  0.0 66.0 jit_solution(5085660669575568203)
XLA Ops:
  0.0 0.0 copy-start.5
  0.0 0.0 copy-start.1
  0.0 0.0 copy-start.3
  0.0 0.0 copy-start.2
  0.0 0.0 copy-start.4
  0.0 0.0 copy-start
  0.0 64.5 %gather.1 = (f32[128,128]{1,0:T(8,128)S(1)}, s32[1,1]{1,0:T(1,128)}) custom-call(s32[8,128]{1,0:T(8,128)} %bitcast.20, s32[8,128]{1,0:T(8,128)} %bitcast.21, s32[2048,128]{1,0:T(8,128)} %bitcast.12, s32[32,128]{1,0:T(8,128)} %bitcast.18, s32[32,128]{1,0:T(8,128)} %bitcast.19, s32[1,128]{1,0:T(1,128)} %bitcast.22, f32[32,128]{1,0:T(8,128)} %bitcast.16, ...), custom_call_target="tpu_custom_call" | custom-call | tf_op jit(solution)/shard_map/gather/pallas_call | solution.py:653
  65.1 0.0 copy-done.5
  65.1 0.0 copy-done.1
  65.1 0.0 copy-done.3
  65.1 0.0 copy-done.2
  65.1 0.0 copy-done.4
  65.1 0.0 copy-done
  65.1 0.2 conditional.1
  65.4 0.6 copy.23
Async XLA Ops:
  0.0 65.1 %copy-start.5 = (s32[128]{0:T(128)S(1)}, s32[128]{0:T(128)}, u32[]{:S(2)}) copy-start(s32[128]{0:T(128)} %param.14) | copy-start | bytes 1540
  0.0 65.1 %copy-start.1 = (f32[128,32]{0,1:T(8,128)S(1)}, f32[128,32]{0,1:T(8,128)}, u32[]{:S(2)}) copy-start(f32[128,32]{0,1:T(8,128)} %param.13) | copy-start | bytes 49156
  0.0 65.1 %copy-start.3 = (s32[128,32]{0,1:T(8,128)S(1)}, s32[128,32]{0,1:T(8,128)}, u32[]{:S(2)}) copy-start(s32[128,32]{0,1:T(8,128)} %param.12) | copy-start | bytes 49156
  0.0 65.1 %copy-start.2 = (s32[128,32]{0,1:T(8,128)S(1)}, s32[128,32]{0,1:T(8,128)}, u32[]{:S(2)}) copy-start(s32[128,32]{0,1:T(8,128)} %param.11) | copy-start | bytes 49156
  0.0 65.1 %copy-start.4 = (s32[128,8]{0,1:T(8,128)S(1)}, s32[128,8]{0,1:T(8,128)}, u32[]{:S(2)}) copy-start(s32[128,8]{0,1:T(8,128)} %param.10) | copy-start | bytes 12292
  0.0 65.1 %copy-start = (s32[262144]{0:T(1024)S(1)}, s32[262144]{0:T(1024)}, u32[]{:S(2)}) copy-start(s32[262144]{0:T(1024)} %param.15) | copy-start | bytes 3145732

commit v3 on v2

--- a/solution.py
+++ b/solution.py
@@ -280,7 +280,8 @@
         solution, residual, direction, norm = carry
         d_top = direction.astype(BF16)
         d_rest = (direction - d_top.astype(F32)).astype(BF16)
-        image = direction + (
+        image = direction
+        unobserved_part = (
             jnp.dot(top, d_top, preferred_element_type=F32)
             + jnp.dot(top, d_rest, preferred_element_type=F32)
             + jnp.dot(rest, d_top, preferred_element_type=F32)
@@ -289,6 +290,7 @@
             vector = vectors[item]
             projected = jnp.sum(vector * direction, axis=0, keepdims=True)
             image = image + vector * (weights[item : item + 1, :] * projected)
+        image = image + unobserved_part
         alpha = norm / jnp.sum(direction * image, axis=0, keepdims=True)
         solution = solution + alpha * direction
         residual = residual - alpha * image
@@ -476,7 +478,7 @@
         outgoing[peer] = stage[...].astype(BF16)
 
     def serve(i, carry):
-        gx, gy = shifted(lax.rem(i * 77, shards))
+        gx, gy = shifted(lax.rem(i * (77 - 26 * core_me), shards))
         peer = gx * gy_size + gy
         collect(peer)
         send(outgoing.at[peer], landed.at[my_place], send_sem, recv_sem, (gx, gy), gy_size).start()

time: 66.2 us -> 65.1 us (0.983)
  Pallas kernels: 64.5 us -> 63.4 us
    pallas_call x1, Pallas kernels: 64.5 us -> 63.4 us  [gather(): pl.pallas_call(functools.partial(gather_kernel, shards, gy_size, blocks_d...]
where the time goes in v3:
time: 65.1 us; the launch traced here: 64.9 us
  Pallas kernels  63.4 us (97%)
  local copies, waits for them, and re-layouts  0.66 us (1%)
    pallas_call x1, Pallas kernels, gather(): pl.pallas_call(functools.partial(gather_kernel, shards, gy_size, blocks_d...  63.4 us

profile of v3, /device:TPU:1, one launch (start us, length us, event | category | flops | bytes accessed | tf_op | source)
XLA Modules:
  0.0 64.9 jit_solution(12000868846782154579)
XLA Ops:
  0.0 0.0 copy-start.5
  0.0 0.0 copy-start.1
  0.0 0.0 copy-start.3
  0.0 0.0 copy-start.2
  0.0 0.0 copy-start.4
  0.0 0.0 copy-start
  0.0 63.4 %gather.1 = (f32[128,128]{1,0:T(8,128)S(1)}, s32[1,1]{1,0:T(1,128)}) custom-call(s32[8,128]{1,0:T(8,128)} %bitcast.20, s32[8,128]{1,0:T(8,128)} %bitcast.21, s32[2048,128]{1,0:T(8,128)} %bitcast.12, s32[32,128]{1,0:T(8,128)} %bitcast.18, s32[32,128]{1,0:T(8,128)} %bitcast.19, s32[1,128]{1,0:T(1,128)} %bitcast.22, f32[32,128]{1,0:T(8,128)} %bitcast.16, ...), custom_call_target="tpu_custom_call" | custom-call | tf_op jit(solution)/shard_map/gather/pallas_call | solution.py:655
  64.0 0.0 copy-done.5
  64.0 0.0 copy-done.1
  64.0 0.0 copy-done.3
  64.0 0.0 copy-done.2
  64.0 0.0 copy-done.4
  64.1 0.0 copy-done
  64.1 0.2 conditional.1
  64.3 0.6 copy.23
Async XLA Ops:
  0.0 64.0 %copy-start.5 = (s32[128]{0:T(128)S(1)}, s32[128]{0:T(128)}, u32[]{:S(2)}) copy-start(s32[128]{0:T(128)} %param.14) | copy-start | bytes 1540
  0.0 64.0 %copy-start.1 = (f32[128,32]{0,1:T(8,128)S(1)}, f32[128,32]{0,1:T(8,128)}, u32[]{:S(2)}) copy-start(f32[128,32]{0,1:T(8,128)} %param.13) | copy-start | bytes 49156
  0.0 64.0 %copy-start.3 = (s32[128,32]{0,1:T(8,128)S(1)}, s32[128,32]{0,1:T(8,128)}, u32[]{:S(2)}) copy-start(s32[128,32]{0,1:T(8,128)} %param.12) | copy-start | bytes 49156
  0.0 64.0 %copy-start.2 = (s32[128,32]{0,1:T(8,128)S(1)}, s32[128,32]{0,1:T(8,128)}, u32[]{:S(2)}) copy-start(s32[128,32]{0,1:T(8,128)} %param.11) | copy-start | bytes 49156
  0.0 64.0 %copy-start.4 = (s32[128,8]{0,1:T(8,128)S(1)}, s32[128,8]{0,1:T(8,128)}, u32[]{:S(2)}) copy-start(s32[128,8]{0,1:T(8,128)} %param.10) | copy-start | bytes 12292
  0.0 64.0 %copy-start = (s32[262144]{0:T(1024)S(1)}, s32[262144]{0:T(1024)}, u32[]{:S(2)}) copy-start(s32[262144]{0:T(1024)} %param.15) | copy-start | bytes 3145732

commit v4 on v3

--- a/solution.py
+++ b/solution.py
@@ -520,7 +520,7 @@
         chosen = jnp.where(lane == row_index[:, item : item + 1], spot, 0.0)
         chosen = jnp.sum(chosen, axis=1, keepdims=True)
         spots_now = jnp.where(slot_lane == item, chosen, spots_now)
-    spots[...] = spots_now.astype(jnp.int32)
+    spots[...] = spots_now.astype(jnp.int32) & (CORES * rows_dev - 1)
     top[...] = jnp.max(jnp.max(asked[...], axis=0), axis=1, keepdims=True)
 
     spots_to = pltpu.make_async_copy(spots, spots_here, own_sem.at[0])
@@ -542,8 +542,7 @@
 
     def take(user, carry):
         for item in range(USER_ITEMS):
-            spot = spots_here[user, item] & (CORES * rows_dev - 1)
-            rows[pl.ds(item * users + user, 1), :] = wide[pl.ds(spot, 1), :]
+            rows[pl.ds(item * users + user, 1), :] = wide[pl.ds(spots_here[user, item], 1), :]
         return carry
 
     lax.fori_loop(0, users, take, 0)

time: 65.1 us -> 64.2 us (0.986)
  Pallas kernels: 63.4 us -> 62.4 us
    pallas_call x1, Pallas kernels: 63.4 us -> 62.4 us  [gather(): pl.pallas_call(functools.partial(gather_kernel, shards, gy_size, blocks_d...]
where the time goes in v4:
time: 64.2 us; the launch traced here: 64 us
  Pallas kernels  62.4 us (97%)
  local copies, waits for them, and re-layouts  0.66 us (1%)
  between operations  0.65 us (1%)
    pallas_call x1, Pallas kernels, gather(): pl.pallas_call(functools.partial(gather_kernel, shards, gy_size, blocks_d...  62.4 us

profile of v4, /device:TPU:1, one launch (start us, length us, event | category | flops | bytes accessed | tf_op | source)
XLA Modules:
  0.0 64.0 jit_solution(12205066182365624072)
XLA Ops:
  0.0 0.0 copy-start.5
  0.0 0.0 copy-start.1
  0.0 0.0 copy-start.3
  0.0 0.0 copy-start.2
  0.0 0.0 copy-start.4
  0.0 0.0 copy-start
  0.0 62.4 %gather.1 = (f32[128,128]{1,0:T(8,128)S(1)}, s32[1,1]{1,0:T(1,128)}) custom-call(s32[8,128]{1,0:T(8,128)} %bitcast.20, s32[8,128]{1,0:T(8,128)} %bitcast.21, s32[2048,128]{1,0:T(8,128)} %bitcast.12, s32[32,128]{1,0:T(8,128)} %bitcast.18, s32[32,128]{1,0:T(8,128)} %bitcast.19, s32[1,128]{1,0:T(1,128)} %bitcast.22, f32[32,128]{1,0:T(8,128)} %bitcast.16, ...), custom_call_target="tpu_custom_call" | custom-call | tf_op jit(solution)/shard_map/gather/pallas_call | solution.py:654
  63.1 0.0 copy-done.5
  63.1 0.0 copy-done.1
  63.1 0.0 copy-done.3
  63.1 0.0 copy-done.2
  63.1 0.0 copy-done.4
  63.1 0.0 copy-done
  63.1 0.2 conditional.1
  63.4 0.6 copy.23
Async XLA Ops:
  0.0 63.1 %copy-start.5 = (s32[128]{0:T(128)S(1)}, s32[128]{0:T(128)}, u32[]{:S(2)}) copy-start(s32[128]{0:T(128)} %param.14) | copy-start | bytes 1540
  0.0 63.1 %copy-start.1 = (f32[128,32]{0,1:T(8,128)S(1)}, f32[128,32]{0,1:T(8,128)}, u32[]{:S(2)}) copy-start(f32[128,32]{0,1:T(8,128)} %param.13) | copy-start | bytes 49156
  0.0 63.1 %copy-start.3 = (s32[128,32]{0,1:T(8,128)S(1)}, s32[128,32]{0,1:T(8,128)}, u32[]{:S(2)}) copy-start(s32[128,32]{0,1:T(8,128)} %param.12) | copy-start | bytes 49156
  0.0 63.1 %copy-start.2 = (s32[128,32]{0,1:T(8,128)S(1)}, s32[128,32]{0,1:T(8,128)}, u32[]{:S(2)}) copy-start(s32[128,32]{0,1:T(8,128)} %param.11) | copy-start | bytes 49156
  0.0 63.1 %copy-start.4 = (s32[128,8]{0,1:T(8,128)S(1)}, s32[128,8]{0,1:T(8,128)}, u32[]{:S(2)}) copy-start(s32[128,8]{0,1:T(8,128)} %param.10) | copy-start | bytes 12292
  0.0 63.1 %copy-start = (s32[262144]{0:T(1024)S(1)}, s32[262144]{0:T(1024)}, u32[]{:S(2)}) copy-start(s32[262144]{0:T(1024)} %param.15) | copy-start | bytes 3145732
